TPU v7x, 32 devices: a whole 2x2x4 slice. The times are simulated.
32 devices in a mesh: grp: 4 (over x, core), shard: 8 (over z, y).
Axes of the slice: x: 2, y: 2, z: 4, core: 2. Of those that a mesh axis runs over, the one named last changes fastest.
Arguments:
- acts: bfloat16 [3, 4096, 4096], P(None, ('grp', 'shard')), may hold values from -6 to 6
- hidden: bfloat16 [4096, 7168], P(('grp', 'shard')), may hold values from -6 to 6
- grads: bfloat16 [4096, 28672], P(('grp', 'shard')), may hold values from -0.14941406 to 0.14941406
- bases_main: bfloat16 [6, 4096, 256], P(None, 'shard'), may hold values from -0.09375 to 0.09375
- bases_down: bfloat16 [7168, 256], P('shard'), may hold values from -0.0625 to 0.0625
- moment_first: float32 [256, 28672], P(None, 'shard'), may hold values from -6 to 6
- moment_second: float32 [256, 28672], P(None, 'shard'), may hold values from 1 to 16
Outputs:
- new_first: float32 [256, 28672], P(None, 'shard')
- new_second: float32 [256, 28672], P(None, 'shard')
- upd_query: bfloat16 [4096, 4096], P(None, 'shard')
- upd_key: bfloat16 [4096, 1024], P(None, 'shard')
- upd_value: bfloat16 [4096, 1024], P(None, 'shard')
- upd_output: bfloat16 [4096, 4096], P(None, 'shard')
- upd_gate: bfloat16 [4096, 7168], P(None, 'shard')
- upd_up: bfloat16 [4096, 7168], P(None, 'shard')
- upd_down: bfloat16 [7168, 4096], P(None, 'shard')
All inputs are finite; a program needn't handle non-finite values.
Results may differ from a plain program's by a relative error of at most 0.02.
Values may be sent and summed in bfloat16 or wider, within the bound.
A program may use at most 192 MiB of HBM per device.

v0:
```python
import jax
import jax.numpy as jnp
from jax import lax
from jax.sharding import PartitionSpec as P

D = 4096
KV = 1024
FF = 7168
STEP = 1000


beta_first = 0.9
beta_second = 0.999
adam_epsilon = 1e-08


def column_runs():
    widths = (D, KV, KV, D, FF, FF, D)
    starts = []
    position = 0
    for width in widths:
        starts.append(position)
        position = position + width
    return (widths, starts)


def adam_moments(gradient, first, second):
    updated_first = beta_first * first + (1.0 - beta_first) * gradient
    updated_second = beta_second * second + (1.0 - beta_second) * gradient * gradient
    return (updated_first, updated_second)


def local(acts, hidden, grads, bases_main, bases_down, moment_first, moment_second):
    widths, starts = column_runs()
    sources = (0, 0, 0, 1, 2, 2)
    n_shard = lax.axis_size("shard")
    rank = bases_main.shape[2]
    full_main, full_down = (
        lax.all_gather(bases_main, "shard", axis=1, tiled=True),
        lax.all_gather(bases_down[None], "shard", axis=1, tiled=True),
    )
    full_down = full_down[0]

    def basis_of(matrix):
        return full_down if matrix == 6 else full_main[matrix]

    blocks = []
    for matrix in range(7):
        source = hidden if matrix == 6 else acts[sources[matrix]]
        partial_term = jnp.dot(
            jnp.dot(source, basis_of(matrix), preferred_element_type=jnp.float32)
            .astype(jnp.bfloat16)
            .T,
            grads[:, starts[matrix] : starts[matrix] + widths[matrix]],
            preferred_element_type=jnp.float32,
        )
        blocks.append(partial_term.reshape(rank, n_shard, widths[matrix] // n_shard))
    stacked = jnp.concatenate(blocks, axis=2)
    shard_sum = lax.psum_scatter(
        stacked.astype(jnp.bfloat16), "shard", scatter_dimension=1, tiled=True
    ).astype(jnp.float32)[:, 0]
    total = lax.psum(shard_sum.astype(jnp.bfloat16), "grp").astype(jnp.float32)
    new_first, new_second = adam_moments(total, moment_first, moment_second)
    correct_first = 1.0 - beta_first**STEP
    correct_second = 1.0 - beta_second**STEP
    direction = (
        new_first / correct_first / (jnp.sqrt(new_second / correct_second) + adam_epsilon)
    ).astype(jnp.bfloat16)
    updates = []
    for matrix in range(7):
        offset = starts[matrix] // n_shard
        run_width = widths[matrix] // n_shard
        direction_now = direction[:, offset : offset + run_width]
        updates.append(
            jnp.dot(basis_of(matrix), direction_now, preferred_element_type=jnp.float32).astype(
                jnp.bfloat16
            )
        )
    return (
        new_first,
        new_second,
        updates[0],
        updates[1],
        updates[2],
        updates[3],
        updates[4],
        updates[5],
        updates[6],
    )


def solution(mesh):
    return jax.shard_map(
        local,
        mesh=mesh,
        in_specs=(
            P(None, ("grp", "shard"), None),
            P(("grp", "shard"), None),
            P(("grp", "shard"), None),
            P(None, "shard", None),
            P("shard", None),
            P(None, "shard"),
            P(None, "shard"),
        ),
        out_specs=(
            P(None, "shard"),
            P(None, "shard"),
            P(None, "shard"),
            P(None, "shard"),
            P(None, "shard"),
            P(None, "shard"),
            P(None, "shard"),
            P(None, "shard"),
            P(None, "shard"),
        ),
        check_vma=False,
    )
```

profile of v0, /device:TPU:11, one launch (start us, length us, event | category | flops | bytes accessed | tf_op | source)
XLA Modules:
  0.0 684.1 jit_solution(17448855548960992281)
XLA Ops:
  7.2 0.0 copy-start
  7.2 0.0 all-gather.6.cloned.1.call-start
  7.2 0.7 all-gather.6.cloned.1.call-update
  7.9 0.0 all-gather.4.cloned.1.call-start
  8.0 0.7 all-gather.4.cloned.1.call-update
  8.7 0.0 reduce-scatter.2.cloned.1.call-start
  8.7 67.9 %all-gather.6.cloned.1.call-done = bf16[7168,256]{1,0:T(8,128)(2,1)} async-done(((bf16[896,256]{1,0:T(8,128)(2,1)}), bf16[7168,256]{1,0:T(8,128)(2,1)}) %all-gather.6.cloned.1.call-update) | async-done | bytes 3670032 | tf_op jit(solution)/shard_map/all_gather | solution.py:40
  76.6 0.0 copy-done
  76.6 5.9 convolution_convert_fusion.5
  82.5 170.5 %all-gather.4.cloned.1.call-done = bf16[6,4096,256]{2,1,0:T(8,128)(2,1)} async-done(((bf16[6,512,256]{2,1,0:T(8,128)(2,1)}), bf16[6,4096,256]{2,1,0:T(8,128)(2,1)}) %all-gather.4.cloned.1.call-update) | async-done | bytes 12582928 | tf_op jit(solution)/shard_map/all_gather | solution.py:39
  253.0 5.2 convolution_convert_fusion.7
  258.2 3.2 bitcast_dynamic-update-slice_fusion.4
  261.4 2.9 fusion.15
  264.3 0.9 bitcast_dynamic-update-slice_fusion.6
  265.2 2.9 fusion.16
  268.1 1.0 bitcast_dynamic-update-slice_fusion.5
  269.1 5.2 convolution_convert_fusion.6
  274.3 3.2 bitcast_dynamic-update-slice_fusion.3
  277.5 6.4 convolution_convert_fusion.2
  283.9 4.4 bitcast_dynamic-update-slice_fusion.1
  288.3 6.4 convolution_convert_fusion.1
  294.6 0.0 copy-start.2
  294.6 4.6 bitcast_dynamic-update-slice_fusion
  299.2 0.0 copy-done.2
  299.2 1.5 bitcast_dynamic-update-slice_fusion.2
  300.7 0.0 reduce-scatter.2.cloned.1.call-update
  300.8 0.2 all-reduce.2.cloned.1.call-start
  301.0 235.1 %reduce-scatter.2.cloned.1.call-done = bf16[256,1,3584]{2,0,1:T(8,128)(2,1)} async-done(((bf16[256,8,3584]{2,0,1:T(8,128)(2,1)}), bf16[256,1,3584]{2,0,1:T(8,128)(2,1)}) %reduce-scatter.2.cloned.1.call-update) | async-done | bytes 1835024 | tf_op jit(solution)/shard_map/reduce_scatter | solution.py:59
  536.1 0.0 all-reduce.2.cloned.1.call-update
  536.1 49.5 %all-reduce.2.cloned.1.call-done = bf16[256,3584]{1,0:T(8,128)(2,1)} async-done(((bf16[256,3584]{1,0:T(8,128)(2,1)}), bf16[256,3584]{1,0:T(8,128)(2,1)}) %all-reduce.2.cloned.1.call-update) | async-done | bytes 1835024 | tf_op jit(solution)/shard_map/psum | solution.py:62
  585.6 9.0 %divide_convert_fusion = (bf16[256,3584]{1,0:T(8,128)(2,1)S(1)}, f32[256,3584]{1,0:T(8,128)}, f32[256,3584]{1,0:T(8,128)}) fusion(bf16[256,3584]{1,0:T(8,128)(2,1)} %all-reduce.2.cloned.1.call-done, f32[256,3584]{1,0:T(8,128)} %param.13, f32[256,3584]{1,0:T(8,128)} %param.12), kind=kLoop, calls=%fused_computation.23 | loop fusion | flops 11010048 | bytes 18350080 | tf_op jit(solution)/shard_map/convert_element_type | solution.py:68
  594.6 4.9 fusion.1
  599.6 6.4 copy.23
  606.0 2.4 fusion.3
  608.4 1.3 copy.24
  609.7 2.4 fusion.4
  612.1 1.3 copy.25
  613.4 4.9 fusion.2
  618.3 6.4 copy.26
  624.7 6.8 convert_bitcast_fusion.1
  631.5 10.8 %copy.27 = bf16[4096,896]{1,0:T(8,128)(2,1)} copy(bf16[4096,896]{0,1:T(8,128)(2,1)} %convert_bitcast_fusion.1) | data formatting | bytes 14680064
  642.3 6.8 convert_bitcast_fusion
  649.1 10.8 %copy.28 = bf16[4096,896]{1,0:T(8,128)(2,1)} copy(bf16[4096,896]{0,1:T(8,128)(2,1)} %convert_bitcast_fusion) | data formatting | bytes 14680064
  659.9 7.1 %fusion = bf16[7168,512]{0,1:T(8,128)(2,1)} fusion(bf16[7168,256]{1,0:T(8,128)(2,1)} %all-gather.6.cloned.1.call-done, bf16[256,3584]{1,0:T(8,128)(2,1)S(1)} %get-tuple-element.18), kind=kOutput, calls=%fused_computation.1 | convolution fusion | flops 1882718208 | bytes 11272192 | tf_op jit(solution)/shard_map/dot_general | solution.py:75
  667.0 0.0 copy-start.1
  667.0 10.5 %copy.29 = bf16[7168,512]{1,0:T(8,128)(2,1)} copy(bf16[7168,512]{0,1:T(8,128)(2,1)} %fusion) | data formatting | bytes 14680064
  677.5 0.0 copy-done.1
Async XLA Ops:
  7.2 69.4 %copy-start = (bf16[128,7168]{1,0:T(8,128)(2,1)S(1)}, bf16[128,7168]{1,0:T(8,128)(2,1)}, u32[]{:S(2)}) copy-start(bf16[128,7168]{1,0:T(8,128)(2,1)} %param.8) | copy-start | bytes 5505028
  7.2 69.4 %all-gather.6.cloned.1.call-start = ((), (), s32[]{:S(2)}) async-start(), calls=%async_computation.4 | async-start | bytes 4128768 | tf_op jit(solution)/shard_map/all_gather | solution.py:40
  7.9 245.1 %all-gather.4.cloned.1.call-start = ((), (), s32[]{:S(2)}) async-start(), calls=%async_computation.1 | async-start | bytes 14155776 | tf_op jit(solution)/shard_map/all_gather | solution.py:39
  8.7 527.4 %reduce-scatter.2.cloned.1.call-start = ((), (), s32[]{:S(2)}) async-start(), calls=%async_computation.2 | async-start | bytes 16515072 | tf_op jit(solution)/shard_map/reduce_scatter | solution.py:59
  294.6 4.6 copy-start.2
  300.8 284.8 %all-reduce.2.cloned.1.call-start = ((), (), s32[]{:S(2)}) async-start(), calls=%async_computation.3 | async-start | bytes 3670016 | tf_op jit(solution)/shard_map/psum | solution.py:62
  667.0 10.5 %copy-start.1 = (bf16[128,7168]{1,0:T(8,128)(2,1)S(1)}, bf16[128,7168]{1,0:T(8,128)(2,1)}, u32[]{:S(2)}) copy-start(bf16[128,7168]{1,0:T(8,128)(2,1)} %param.8) | copy-start | bytes 5505028
Sparse Core Ops, SparseCore 0:
  10.2 66.3 all-gather.5
  78.8 174.2 all-gather.3
  300.9 235.1 reduce-scatter.1
  538.3 47.2 all-reduce.1
where the time goes:
time: 688 us; the launch traced here: 684 us
  waiting for transfers between devices  524 us (76%)
  matrix products  70.1 us (10%)
  local copies, waits for them, and re-layouts  66.5 us (10%)
  between operations  13.8 us (2%)
  other arithmetic  9.05 us (1%)
    reduce_scatter x1, waiting for transfers between devices, local(): lax.psum_scatter(stacked.astype(jnp.bfloat16), 'shard', scatter_dimension...  235 us
    all_gather x1, waiting for transfers between devices, local(): lax.all_gather(bases_main, 'shard', axis=1, tiled=True)  171 us
    all_gather x1, waiting for transfers between devices, local(): lax.all_gather(bases_down[None], 'shard', axis=1, tiled=True)  67.9 us
    unnamed x19, local copies, waits for them, and re-layouts  64.9 us
    psum x1, waiting for transfers between devices, local(): total = lax.psum(shard_sum.astype(jnp.bfloat16), 'grp').astype(jnp.float32)  49.5 us
    dot_general x7, matrix products, local(): jnp.dot(basis_of(matrix), direction_now, preferred_element_type=jnp.float32)  35.3 us
    dot_general x7, matrix products, local(): jnp.dot(jnp.dot(source, basis_of(matrix), preferred_element_type=jnp.floa...  34.8 us
  transfers between devices with their start and end apart: 4, of which 4 were waited for; matrix products, arithmetic and copies ran while one was open for 1% of the time, Pallas kernels for 0%

commit v1 on v0

--- a/solution.py
+++ b/solution.py
@@ -1,7 +1,13 @@
+import functools
+
 import jax
 import jax.numpy as jnp
 from jax import lax
+from jax.experimental import pallas as pl
+from jax.experimental.pallas import tpu as pltpu
 from jax.sharding import PartitionSpec as P
+
+MESH = pl.DeviceIdType.MESH
 
 D = 4096
 KV = 1024
@@ -30,7 +36,7 @@
     return (updated_first, updated_second)
 
 
-def local(acts, hidden, grads, bases_main, bases_down, moment_first, moment_second):
+def local_general(acts, hidden, grads, bases_main, bases_down, moment_first, moment_second):
     widths, starts = column_runs()
     sources = (0, 0, 0, 1, 2, 2)
     n_shard = lax.axis_size("shard")
@@ -89,7 +95,345 @@
     )
 
 
+WIDTHS, STARTS = column_runs()
+SOURCES = (0, 0, 0, 1, 2, 2)
+ORDER = (6, 4, 5, 0, 3, 1, 2)
+PIECES = (
+    ((4, 0, 896, 0, 0),),
+    ((5, 0, 896, 0, 0),),
+    ((0, 0, 512, 0, 0), (3, 4096, 384, 512, 0)),
+    ((6, 0, 512, 0, 0), (1, 4096, 128, 512, 0), (2, 5120, 128, 640, 0), (3, 6144, 128, 768, 384)),
+)
+N_SH = 8
+N_GR = 4
+QCOL = 7168
+BCOL = 896
+TOK = 128
+RANK = 256
+
+
+def needed_by(matrix):
+    return [t for t in range(N_GR) if any(piece[0] == matrix for piece in PIECES[t])]
+
+
+def gather_reduce(
+    acts, hidden, grads, bmain, bdown,
+    out_main, out_down, out_g,
+    pm, pd, av, hv, gx, pj, term, ybuf, zbuf, gfin,
+    lsem, osem, zs, zr, ys, yr, cs, cr, gs, gr, js, jr, rys, ryr, rzs, rzr, fs, fr,
+):
+    g = lax.axis_index("grp")
+    s = lax.axis_index("shard")
+    core = g % 2
+    cpeer = g + 1 - 2 * core
+    ypeer = s + 1 - 2 * (s % 2)
+
+    acts_in = pltpu.make_async_copy(acts, av, lsem.at[0])
+    hid_in = pltpu.make_async_copy(hidden, hv, lsem.at[1])
+    acts_in.start()
+    hid_in.start()
+    own_in = []
+    for k in range(7):
+        if k < 6:
+            src = bmain.at[k]
+            dst = pm.at[k, pl.ds(pl.multiple_of(s * 512, 512), 512)]
+        else:
+            src = bdown
+            dst = pd.at[pl.ds(pl.multiple_of(s * 896, 128), 896)]
+        own_in.append(pltpu.make_async_copy(src, dst, lsem.at[2 + k]))
+        own_in[-1].start()
+
+    barrier = pltpu.get_barrier_semaphore()
+    for d in range(1, N_GR):
+        pl.semaphore_signal(barrier, inc=1, device_id=((g + d) % N_GR, s), device_id_type=MESH)
+    for d in range(1, 4):
+        pl.semaphore_signal(barrier, inc=1, device_id=(g, (s + 2 * d) % N_SH), device_id_type=MESH)
+    pl.semaphore_signal(barrier, inc=1, device_id=(g, ypeer), device_id_type=MESH)
+    pl.semaphore_wait(barrier, 7)
+
+    def remote(src, dst, send, recv, grp, shard):
+        return pltpu.make_async_remote_copy(
+            src_ref=src, dst_ref=dst, send_sem=send, recv_sem=recv,
+            device_id=(grp, shard), device_id_type=MESH,
+        )
+
+    def full(k, owner, half):
+        if k < 6:
+            return pm.at[k, pl.ds(pl.multiple_of(owner * 512 + half * 256, 256), 256)]
+        return pd.at[pl.ds(pl.multiple_of(owner * 896 + half * 448, 64), 448)]
+
+    def own(k):
+        if k < 6:
+            return bmain.at[k, pl.ds(pl.multiple_of(core * 256, 256), 256)]
+        return bdown.at[pl.ds(pl.multiple_of(core * 448, 64), 448)]
+
+    pending = []
+    def send_own(k):
+        c = remote(own(k), full(k, s, core), ys.at[k, 0], yr.at[k, 0], g, ypeer)
+        c.start()
+        pending.append(c)
+        for d in (1, 3, 2):
+            c = remote(own(k), full(k, s, core), zs.at[k, d - 1], zr.at[k, d - 1], g, (s + 2 * d) % N_SH)
+            c.start()
+            pending.append(c)
+
+    def send_grads(t):
+        for k, base, width, _, first in PIECES[t]:
+            if width * N_SH == WIDTHS[k]:
+                cuts = [(STARTS[k], base, WIDTHS[k])]
+            else:
+                run = WIDTHS[k] // N_SH
+                cuts = [(STARTS[k] + b * run + first, base + b * width, width) for b in range(N_SH)]
+            for a, b, w in cuts:
+                @pl.when(g != t)
+                def _():
+                    remote(
+                        grads.at[:, pl.ds(a, w)], gx.at[g, :, pl.ds(b, w)], gs.at[t], gr.at[g], t, s
+                    ).start()
+
+                @pl.when(g == t)
+                def _():
+                    pltpu.make_async_copy(
+                        grads.at[:, pl.ds(a, w)], gx.at[t, :, pl.ds(b, w)], gr.at[t]
+                    ).start()
+
+    send_own(ORDER[0])
+    for t in range(N_GR):
+        send_grads(t)
+    for k in ORDER[1:]:
+        send_own(k)
+
+    def after_z(k):
+        for d in (1, 3, 2):
+            owner = (s + N_SH - 2 * d) % N_SH
+            block = full(k, owner, core)
+            remote(block, block, zs.at[k, d - 1], zr.at[k, d - 1], g, ypeer).wait_recv()
+            c = remote(block, block, ys.at[k, d], yr.at[k, d], g, ypeer)
+            c.start()
+            pending.append(c)
+            c = remote(block, block, cs.at[k, d - 1], cr.at[k, d - 1], cpeer, s)
+            c.start()
+            pending.append(c)
+
+    def after_y(k):
+        for d in (0, 1, 3, 2):
+            owner = (ypeer + N_SH - 2 * d) % N_SH
+            block = full(k, owner, core)
+            remote(block, block, ys.at[k, d], yr.at[k, d], g, ypeer).wait_recv()
+            c = remote(block, block, cs.at[k, 3 + d], cr.at[k, 3 + d], cpeer, s)
+            c.start()
+            pending.append(c)
+
+    outs = []
+
+    def project(k):
+        for d in range(1, 4):
+            block = full(k, (s + N_SH - 2 * d) % N_SH, 1 - core)
+            remote(block, block, cs.at[k, d - 1], cr.at[k, d - 1], cpeer, s).wait_recv()
+        for d in range(4):
+            block = full(k, (ypeer + N_SH - 2 * d) % N_SH, 1 - core)
+            remote(block, block, cs.at[k, 3 + d], cr.at[k, 3 + d], cpeer, s).wait_recv()
+        own_in[k].wait()
+        if k < 6:
+            c = pltpu.make_async_copy(pm.at[k], out_main.at[k], osem.at[k])
+        else:
+            c = pltpu.make_async_copy(pd, out_down, osem.at[k])
+        c.start()
+        outs.append(c)
+        x = hv[...] if k == 6 else av[SOURCES[k]]
+        p = pd[...] if k == 6 else pm[k]
+        pj[k, g] = jnp.dot(x, p, preferred_element_type=jnp.float32).astype(jnp.bfloat16)
+        for t in needed_by(k):
+            slot = needed_by(k).index(t)
+
+            @pl.when(g != t)
+            def _():
+                remote(pj.at[k, g], pj.at[k, g], js.at[k, slot], jr.at[k, g], t, s).start()
+
+    acts_waited = False
+    for step in range(len(ORDER) + 2):
+        if step < len(ORDER):
+            after_z(ORDER[step])
+        if 1 <= step < len(ORDER) + 1:
+            after_y(ORDER[step - 1])
+        if step >= 2:
+            if not acts_waited:
+                acts_in.wait()
+                hid_in.wait()
+                acts_waited = True
+            project(ORDER[step - 2])
+
+    for src in range(N_GR):
+        pltpu.make_async_copy(gx.at[src], gx.at[src], gr.at[src]).wait()
+
+    def block_term(t, target):
+        for k, base, width, place, _ in PIECES[t]:
+            left = pj[k].reshape(N_GR * TOK, RANK)
+            cols = pl.ds(pl.multiple_of(base + target * width, 128), width)
+            right = gx[:, :, cols].reshape(N_GR * TOK, width)
+            value = lax.dot_general(
+                left, right, (((0,), (0,)), ((), ())), preferred_element_type=jnp.float32
+            )
+            term[target, :, place : place + width] = value.astype(jnp.bfloat16)
+
+    for t in range(N_GR):
+        @pl.when(g == t)
+        def _():
+            for k, *_ in PIECES[t]:
+                for src in range(N_GR):
+                    if src != t:
+                        remote(
+                            pj.at[k, src], pj.at[k, src], js.at[k, 0], jr.at[k, src], g, ypeer
+                        ).wait_recv()
+
+            def far(d, carry):
+                target = (ypeer + 2 * d) % N_SH
+                block_term(t, target)
+                remote(
+                    term.at[target], ybuf.at[d % 4], rys.at[d % 4], ryr.at[d % 4], g, ypeer
+                ).start()
+                return carry
+
+            lax.fori_loop(1, 5, far, 0)
+
+            def near(d, carry):
+                block_term(t, (s + 2 * d) % N_SH)
+                return carry
+
+            lax.fori_loop(1, 5, near, 0)
+
+    for d in (1, 2, 3, 0):
+        target = (s + 2 * d) % N_SH
+        remote(ybuf.at[d], ybuf.at[d], rys.at[d], ryr.at[d], g, ypeer).wait_recv()
+        total = term[target].astype(jnp.float32) + ybuf[d].astype(jnp.float32)
+        if d:
+            term[target] = total.astype(jnp.bfloat16)
+            c = remote(term.at[target], zbuf.at[d - 1], rzs.at[d - 1], rzr.at[d - 1], g, target)
+            c.start()
+            pending.append(c)
+    for d in (1, 2, 3):
+        remote(zbuf.at[d - 1], zbuf.at[d - 1], rzs.at[d - 1], rzr.at[d - 1], g, ypeer).wait_recv()
+        total = total + zbuf[d - 1].astype(jnp.float32)
+    gfin[...] = total.astype(jnp.bfloat16)
+    keep = pltpu.make_async_copy(gfin, out_g.at[g], osem.at[7])
+    for d in (2, 3, 1):
+        c = remote(gfin, out_g.at[g], fs.at[d - 1], fr.at[d - 1], (g + d) % N_GR, s)
+        c.start()
+        pending.append(c)
+    keep.start()
+    for d in (1, 2, 3):
+        got = out_g.at[(g + N_GR - d) % N_GR]
+        remote(got, got, fs.at[d - 1], fr.at[d - 1], g, ypeer).wait_recv()
+    keep.wait()
+
+    for c in pending:
+        c.wait_send()
+    for d in range(4):
+        remote(ybuf.at[d], ybuf.at[d], rys.at[d], ryr.at[d], g, ypeer).wait_send()
+    for t in range(N_GR):
+        @pl.when(g != t)
+        def _():
+            remote(gx.at[t], gx.at[t], gs.at[t], gr.at[t], t, s).wait_send()
+            for k in range(7):
+                if t in needed_by(k):
+                    slot = needed_by(k).index(t)
+                    remote(pj.at[k, t], pj.at[k, t], js.at[k, slot], jr.at[k, t], t, s).wait_send()
+    for c in outs:
+        c.wait()
+
+
+def moments_and_updates(g4, m1, m2, bm, bd, n1, n2, *rest):
+    updates, direction = rest[:7], rest[7]
+
+    @pl.when(pl.program_id(0) == 0)
+    def _():
+        correct_first = 1.0 - beta_first**STEP
+        correct_second = 1.0 - beta_second**STEP
+        for t in range(N_GR):
+            for k, _b, width, place, first in PIECES[t]:
+                a = STARTS[k] // N_SH + first
+                for c in range(0, width, 128):
+                    cols = slice(a + c, a + c + 128)
+                    gradient = g4[t, :, place + c : place + c + 128].astype(jnp.float32)
+                    new_first, new_second = adam_moments(gradient, m1[:, cols], m2[:, cols])
+                    n1[:, cols] = new_first
+                    n2[:, cols] = new_second
+                    direction[:, cols] = (
+                        new_first / correct_first
+                        / (jnp.sqrt(new_second / correct_second) + adam_epsilon)
+                    ).astype(jnp.bfloat16)
+
+    for k in range(7):
+        a = STARTS[k] // N_SH
+        w = WIDTHS[k] // N_SH
+        basis = bd[...] if k == 6 else bm[k]
+        updates[k][...] = jnp.dot(
+            basis, direction[:, a : a + w], preferred_element_type=jnp.float32
+        ).astype(jnp.bfloat16)
+
+
+def local_block(acts, hidden, grads, bases_main, bases_down, moment_first, moment_second):
+    bf, f32 = jnp.bfloat16, jnp.float32
+    anyspace = pl.BlockSpec(memory_space=pl.ANY)
+    dma = pltpu.SemaphoreType.DMA
+    full_main, full_down, g4 = pl.pallas_call(
+        gather_reduce,
+        out_shape=(
+            jax.ShapeDtypeStruct((6, D, RANK), bf),
+            jax.ShapeDtypeStruct((FF, RANK), bf),
+            jax.ShapeDtypeStruct((N_GR, RANK, BCOL), bf),
+        ),
+        in_specs=[anyspace] * 5,
+        out_specs=(anyspace,) * 3,
+        scratch_shapes=[
+            pltpu.VMEM((6, D, RANK), bf),
+            pltpu.VMEM((FF, RANK), bf),
+            pltpu.VMEM((3, TOK, D), bf),
+            pltpu.VMEM((TOK, FF), bf),
+            pltpu.VMEM((N_GR, TOK, QCOL), bf),
+            pltpu.VMEM((7, N_GR, TOK, RANK), bf),
+            pltpu.VMEM((N_SH, RANK, BCOL), bf),
+            pltpu.VMEM((4, RANK, BCOL), bf),
+            pltpu.VMEM((3, RANK, BCOL), bf),
+            pltpu.VMEM((RANK, BCOL), bf),
+            dma((9,)), dma((8,)),
+            dma((7, 3)), dma((7, 3)), dma((7, 4)), dma((7, 4)), dma((7, 7)), dma((7, 7)),
+            dma((4,)), dma((4,)), dma((7, 2)), dma((7, 4)),
+            dma((4,)), dma((4,)), dma((3,)), dma((3,)), dma((3,)), dma((3,)),
+        ],
+        compiler_params=pltpu.CompilerParams(
+            collective_id=0, has_side_effects=True, vmem_limit_bytes=56 * 2**20
+        ),
+    )(acts, hidden, grads, bases_main, bases_down)
+
+    steps = 8
+    cols = moment_first.shape[1]
+    once = pl.Buffered(1)
+    whole = lambda: pl.BlockSpec((RANK, cols), lambda i: (0, 0), pipeline_mode=once)
+    runs = [w // N_SH for w in WIDTHS]
+    rows = [FF if k == 6 else D for k in range(7)]
+    return pl.pallas_call(
+        moments_and_updates,
+        grid=(steps,),
+        out_shape=[jax.ShapeDtypeStruct((RANK, cols), f32)] * 2
+        + [jax.ShapeDtypeStruct((rows[k], runs[k]), bf) for k in range(7)],
+        in_specs=[
+            pl.BlockSpec((N_GR, RANK, BCOL), lambda i: (0, 0, 0), pipeline_mode=once),
+            whole(),
+            whole(),
+            pl.BlockSpec((6, D // steps, RANK), lambda i: (0, i, 0)),
+            pl.BlockSpec((FF // steps, RANK), lambda i: (i, 0)),
+        ],
+        out_specs=[whole(), whole()]
+        + [pl.BlockSpec((rows[k] // steps, runs[k]), lambda i: (i, 0)) for k in range(7)],
+        scratch_shapes=[pltpu.VMEM((RANK, cols), bf)],
+        compiler_params=pltpu.CompilerParams(vmem_limit_bytes=56 * 2**20),
+    )(g4, moment_first, moment_second, full_main, full_down)
+
+
 def solution(mesh):
+    block = mesh.shape["grp"] == N_GR and mesh.shape["shard"] == N_SH
+    local = local_block if block else local_general
     return jax.shard_map(
         local,
         mesh=mesh,

time: 688 us -> 213 us (0.31)
  waiting for transfers between devices: 524 us -> 0 us
  Pallas kernels: 0 us -> 212 us
  matrix products: 70.1 us -> 0 us
  local copies, waits for them, and re-layouts: 66.5 us -> 0 us
  between operations: 13.8 us -> 0.72 us
  other arithmetic: 9.05 us -> 0 us
    all_gather x2 -> x0, waiting for transfers between devices: 238 us -> none  [the longest x1 171 us: local(): lax.all_gather(bases_main, 'shard', axis=1, tiled=True)]
    reduce_scatter x1 -> x0, waiting for transfers between devices: 235 us -> none  [local(): lax.psum_scatter(stacked.astype(jnp.bfloat16), 'shard', scatter_dimension...]
    pallas_call x0 -> x2, Pallas kernels: none -> 212 us  [the longest x1 184 us: local_block(): pl.pallas_call(gather_reduce, out_shape=(jax.ShapeDtypeStruct((6, D, RANK...]
    dot_general x14 -> x0, matrix products: 70.1 us -> none  [the longest x7 35.3 us: local(): jnp.dot(basis_of(matrix), direction_now, preferred_element_type=jnp.float32)]
    unnamed x19 -> x0, local copies, waits for them, and re-layouts: 64.9 us -> none
    psum x1 -> x0, waiting for transfers between devices: 49.5 us -> none  [local(): total = lax.psum(shard_sum.astype(jnp.bfloat16), 'grp').astype(jnp.float32)]
    convert_element_type x1 -> x0, other arithmetic: 9.05 us -> none  [local(): direction = (new_first / correct_first / (jnp.sqrt(new_second / correct_s...]
  transfers between devices with their start and end apart: 4 -> 0, of which waited for: 4 -> 0; matrix products, arithmetic and copies ran while one was open for 1% -> 0% of each run, Pallas kernels for 0% -> 0%
where the time goes in v1:
time: 213 us
  Pallas kernels  212 us (100%)
    pallas_call x1, Pallas kernels, local_block(): pl.pallas_call(gather_reduce, out_shape=(jax.ShapeDtypeStruct((6, D, RANK...  184 us
    pallas_call x1, Pallas kernels, local_block(): pl.pallas_call(moments_and_updates, grid=(steps,), out_shape=[jax.ShapeDt...  27.9 us

profile of v1, /device:TPU:11, one launch (start us, length us, event | category | flops | bytes accessed | tf_op | source)
XLA Modules:
  0.0 212.7 jit_solution(2042266828782824145)
XLA Ops:
  0.6 184.0 %shard_map.142 = (bf16[6,4096,256]{2,1,0:T(8,128)(2,1)}, bf16[7168,256]{1,0:T(8,128)(2,1)}, bf16[4,256,896]{2,1,0:T(8,128)(2,1)}) custom-call(bf16[3,128,4096]{2,1,0:T(8,128)(2,1)} %acts.1, bf16[128,7168]{1,0:T(8,128)(2,1)} %hidden.1, bf16[128,28672]{1,0:T(8,128)(2,1)} %grads.1, bf16[6,512,256]{2,1,0:T(8,128)(2,1)} %bmain.1, bf16[896,256]{1,0:T(8,128)(2,1)} %bdown.1), custom_call_target="tpu_custom_call" | custom-call | tf_op jit(solution)/shard_map/pallas_call | solution.py:379
  184.7 27.9 %shard_map.143 = (f32[256,3584]{1,0:T(8,128)}, f32[256,3584]{1,0:T(8,128)}, bf16[4096,512]{1,0:T(8,128)(2,1)}, bf16[4096,128]{1,0:T(8,128)(2,1)}, bf16[4096,128]...) custom-call(bf16[4,256,896]{2,1,0:T(8,128)(2,1)} %get-tuple-element., ...), custom_call_target="tpu_custom_call" | custom-call | tf_op jit(solution)/shard_map/pallas_call | solution.py:415

commit v2 on v1

--- a/solution.py
+++ b/solution.py
@@ -112,14 +112,24 @@
 RANK = 256
 
 
+def adam_direction(gradient, first, second):
+    new_first, new_second = adam_moments(gradient, first, second)
+    correct_first = 1.0 - beta_first**STEP
+    correct_second = 1.0 - beta_second**STEP
+    direction = (
+        new_first / correct_first / (jnp.sqrt(new_second / correct_second) + adam_epsilon)
+    ).astype(jnp.bfloat16)
+    return new_first, new_second, direction
+
+
 def needed_by(matrix):
     return [t for t in range(N_GR) if any(piece[0] == matrix for piece in PIECES[t])]
 
 
 def gather_reduce(
-    acts, hidden, grads, bmain, bdown,
-    out_main, out_down, out_g,
-    pm, pd, av, hv, gx, pj, term, ybuf, zbuf, gfin,
+    acts, hidden, grads, bmain, bdown, first, second,
+    out_main, out_down, out_g, out_dir,
+    pm, pd, av, hv, gx, pj, term, ybuf, zbuf, gall, m1, m2, direction,
     lsem, osem, zs, zr, ys, yr, cs, cr, gs, gr, js, jr, rys, ryr, rzs, rzr, fs, fr,
 ):
     g = lax.axis_index("grp")
@@ -132,6 +142,8 @@
     hid_in = pltpu.make_async_copy(hidden, hv, lsem.at[1])
     acts_in.start()
     hid_in.start()
+    first_in = pltpu.make_async_copy(first, m1, lsem.at[9])
+    second_in = pltpu.make_async_copy(second, m2, lsem.at[10])
     own_in = []
     for k in range(7):
         if k < 6:
@@ -202,6 +214,8 @@
         send_grads(t)
     for k in ORDER[1:]:
         send_own(k)
+    first_in.start()
+    second_in.start()
 
     def after_z(k):
         for d in (1, 3, 2):
@@ -314,17 +328,56 @@
     for d in (1, 2, 3):
         remote(zbuf.at[d - 1], zbuf.at[d - 1], rzs.at[d - 1], rzr.at[d - 1], g, ypeer).wait_recv()
         total = total + zbuf[d - 1].astype(jnp.float32)
-    gfin[...] = total.astype(jnp.bfloat16)
-    keep = pltpu.make_async_copy(gfin, out_g.at[g], osem.at[7])
-    for d in (2, 3, 1):
-        c = remote(gfin, out_g.at[g], fs.at[d - 1], fr.at[d - 1], (g + d) % N_GR, s)
-        c.start()
-        pending.append(c)
+    gall[g] = total.astype(jnp.bfloat16)
+    across = (g + 2) % N_GR
+    diagonal = (cpeer + 2) % N_GR
+    c = remote(gall.at[g], gall.at[g], fs.at[0], fr.at[0], across, s)
+    c.start()
+    pending.append(c)
+    c = remote(gall.at[g], gall.at[g], fs.at[1], fr.at[1], cpeer, s)
+    c.start()
+    pending.append(c)
+    first_in.wait()
+    second_in.wait()
+
+    def direct(quarter):
+        for t in range(N_GR):
+            @pl.when(quarter == t)
+            def _():
+                def chunk(c, carry):
+                    if t == 2:
+                        col = 128 * c + 256 * (c // 4)
+                    elif t == 3:
+                        late = c // 4
+                        col = (1 - late) * (3072 + 128 * c) + late * (128 * c + 384 * (c // 6))
+                    else:
+                        col = 1280 + BCOL * t + 128 * c
+                    cols = pl.ds(pl.multiple_of(col, 128), 128)
+                    gradient = gall[t, :, pl.ds(pl.multiple_of(128 * c, 128), 128)]
+                    _, _, value = adam_direction(
+                        gradient.astype(jnp.float32), m1[:, cols], m2[:, cols]
+                    )
+                    direction[:, cols] = value
+                    return carry
+
+                lax.fori_loop(0, BCOL // 128, chunk, 0)
+
+    direct(g)
+    remote(gall.at[cpeer], gall.at[cpeer], fs.at[1], fr.at[1], cpeer, s).wait_recv()
+    direct(cpeer)
+    remote(gall.at[across], gall.at[across], fs.at[0], fr.at[0], across, s).wait_recv()
+    c = remote(gall.at[across], gall.at[across], fs.at[2], fr.at[2], cpeer, s)
+    c.start()
+    pending.append(c)
+    direct(across)
+    remote(gall.at[diagonal], gall.at[diagonal], fs.at[2], fr.at[2], cpeer, s).wait_recv()
+    keep = pltpu.make_async_copy(gall, out_g, osem.at[7])
     keep.start()
-    for d in (1, 2, 3):
-        got = out_g.at[(g + N_GR - d) % N_GR]
-        remote(got, got, fs.at[d - 1], fr.at[d - 1], g, ypeer).wait_recv()
-    keep.wait()
+    outs.append(keep)
+    direct(diagonal)
+    keep = pltpu.make_async_copy(direction, out_dir, osem.at[8])
+    keep.start()
+    outs.append(keep)
 
     for c in pending:
         c.wait_send()
@@ -342,26 +395,12 @@
         c.wait()
 
 
-def moments_and_updates(g4, m1, m2, bm, bd, n1, n2, *rest):
-    updates, direction = rest[:7], rest[7]
-
-    @pl.when(pl.program_id(0) == 0)
-    def _():
-        correct_first = 1.0 - beta_first**STEP
-        correct_second = 1.0 - beta_second**STEP
-        for t in range(N_GR):
-            for k, _b, width, place, first in PIECES[t]:
-                a = STARTS[k] // N_SH + first
-                for c in range(0, width, 128):
-                    cols = slice(a + c, a + c + 128)
-                    gradient = g4[t, :, place + c : place + c + 128].astype(jnp.float32)
-                    new_first, new_second = adam_moments(gradient, m1[:, cols], m2[:, cols])
-                    n1[:, cols] = new_first
-                    n2[:, cols] = new_second
-                    direction[:, cols] = (
-                        new_first / correct_first
-                        / (jnp.sqrt(new_second / correct_second) + adam_epsilon)
-                    ).astype(jnp.bfloat16)
+def moments_and_updates(g4, m1, m2, direction, bm, bd, n1, n2, *updates):
+    for t in range(N_GR):
+        for k, _b, width, place, first in PIECES[t]:
+            cols = slice(STARTS[k] // N_SH + first, STARTS[k] // N_SH + first + width)
+            gradient = g4[t, :, place : place + width].astype(jnp.float32)
+            n1[:, cols], n2[:, cols] = adam_moments(gradient, m1[:, cols], m2[:, cols])
 
     for k in range(7):
         a = STARTS[k] // N_SH
@@ -376,15 +415,16 @@
     bf, f32 = jnp.bfloat16, jnp.float32
     anyspace = pl.BlockSpec(memory_space=pl.ANY)
     dma = pltpu.SemaphoreType.DMA
-    full_main, full_down, g4 = pl.pallas_call(
+    full_main, full_down, g4, direction = pl.pallas_call(
         gather_reduce,
         out_shape=(
             jax.ShapeDtypeStruct((6, D, RANK), bf),
             jax.ShapeDtypeStruct((FF, RANK), bf),
             jax.ShapeDtypeStruct((N_GR, RANK, BCOL), bf),
+            jax.ShapeDtypeStruct((RANK, moment_first.shape[1]), bf),
         ),
-        in_specs=[anyspace] * 5,
-        out_specs=(anyspace,) * 3,
+        in_specs=[anyspace] * 7,
+        out_specs=(anyspace,) * 4,
         scratch_shapes=[
             pltpu.VMEM((6, D, RANK), bf),
             pltpu.VMEM((FF, RANK), bf),
@@ -395,8 +435,11 @@
             pltpu.VMEM((N_SH, RANK, BCOL), bf),
             pltpu.VMEM((4, RANK, BCOL), bf),
             pltpu.VMEM((3, RANK, BCOL), bf),
-            pltpu.VMEM((RANK, BCOL), bf),
-            dma((9,)), dma((8,)),
+            pltpu.VMEM((N_GR, RANK, BCOL), bf),
+            pltpu.VMEM(moment_first.shape, f32),
+            pltpu.VMEM(moment_first.shape, f32),
+            pltpu.VMEM(moment_first.shape, bf),
+            dma((11,)), dma((9,)),
             dma((7, 3)), dma((7, 3)), dma((7, 4)), dma((7, 4)), dma((7, 7)), dma((7, 7)),
             dma((4,)), dma((4,)), dma((7, 2)), dma((7, 4)),
             dma((4,)), dma((4,)), dma((3,)), dma((3,)), dma((3,)), dma((3,)),
@@ -404,12 +447,12 @@
         compiler_params=pltpu.CompilerParams(
             collective_id=0, has_side_effects=True, vmem_limit_bytes=56 * 2**20
         ),
-    )(acts, hidden, grads, bases_main, bases_down)
+    )(acts, hidden, grads, bases_main, bases_down, moment_first, moment_second)
 
     steps = 8
     cols = moment_first.shape[1]
     once = pl.Buffered(1)
-    whole = lambda: pl.BlockSpec((RANK, cols), lambda i: (0, 0), pipeline_mode=once)
+    band = lambda: pl.BlockSpec((RANK // steps, cols), lambda i: (i, 0))
     runs = [w // N_SH for w in WIDTHS]
     rows = [FF if k == 6 else D for k in range(7)]
     return pl.pallas_call(
@@ -418,17 +461,17 @@
         out_shape=[jax.ShapeDtypeStruct((RANK, cols), f32)] * 2
         + [jax.ShapeDtypeStruct((rows[k], runs[k]), bf) for k in range(7)],
         in_specs=[
-            pl.BlockSpec((N_GR, RANK, BCOL), lambda i: (0, 0, 0), pipeline_mode=once),
-            whole(),
-            whole(),
+            pl.BlockSpec((N_GR, RANK // steps, BCOL), lambda i: (0, i, 0)),
+            band(),
+            band(),
+            pl.BlockSpec((RANK, cols), lambda i: (0, 0), pipeline_mode=once),
             pl.BlockSpec((6, D // steps, RANK), lambda i: (0, i, 0)),
             pl.BlockSpec((FF // steps, RANK), lambda i: (i, 0)),
         ],
-        out_specs=[whole(), whole()]
+        out_specs=[band(), band()]
         + [pl.BlockSpec((rows[k] // steps, runs[k]), lambda i: (i, 0)) for k in range(7)],
-        scratch_shapes=[pltpu.VMEM((RANK, cols), bf)],
         compiler_params=pltpu.CompilerParams(vmem_limit_bytes=56 * 2**20),
-    )(g4, moment_first, moment_second, full_main, full_down)
+    )(g4, moment_first, moment_second, direction, full_main, full_down)
 
 
 def solution(mesh):

time: 213 us -> 204 us (0.958)
  Pallas kernels: 212 us -> 203 us
    pallas_call x1, Pallas kernels: 184 us -> 178 us  [local_block(): pl.pallas_call(gather_reduce, out_shape=(jax.ShapeDtypeStruct((6, D, RANK...]
    pallas_call x1, Pallas kernels: 27.9 us -> 24.8 us  [local_block(): pl.pallas_call(moments_and_updates, grid=(steps,), out_shape=[jax.ShapeDt...]
where the time goes in v2:
time: 204 us; the launch traced here: 203 us
  Pallas kernels  203 us (100%)
    pallas_call x1, Pallas kernels, local_block(): pl.pallas_call(gather_reduce, out_shape=(jax.ShapeDtypeStruct((6, D, RANK...  178 us
    pallas_call x1, Pallas kernels, local_block(): pl.pallas_call(moments_and_updates, grid=(steps,), out_shape=[jax.ShapeDt...  24.8 us

profile of v2, /device:TPU:11, one launch (start us, length us, event | category | flops | bytes accessed | tf_op | source)
XLA Modules:
  0.0 203.4 jit_solution(25400665385781498)
XLA Ops:
  0.6 177.9 %shard_map.142 = (bf16[6,4096,256]{2,1,0:T(8,128)(2,1)}, bf16[7168,256]{1,0:T(8,128)(2,1)}, bf16[4,256,896]{2,1,0:T(8,128)(2,1)}, bf16[256,3584]{1,0:T(8,128)(2,1)}) custom-call(bf16[3,128,4096]{2,1,0:T(8,128)(2,1)} %acts.1, bf16[128,7168]{1,0:T(8,128)(2,1)} %hidden.1, bf16[128,28672]{1,0:T(8,128)(2,1)} %grads.1, bf16[6,512,256]{2,1,0:T(8,128)(2,1)} %bmain.1, ...), custom_call_target="tpu_custom_call" | custom-call | tf_op jit(solution)/shard_map/pallas_call | solution.py:418
  178.5 24.8 %shard_map.143 = (f32[256,3584]{1,0:T(8,128)}, f32[256,3584]{1,0:T(8,128)}, bf16[4096,512]{1,0:T(8,128)(2,1)}, bf16[4096,128]{1,0:T(8,128)(2,1)}, bf16[4096,128]...) custom-call(bf16[4,256,896]{2,1,0:T(8,128)(2,1)} %get-tuple-element., ...), custom_call_target="tpu_custom_call" | custom-call | tf_op jit(solution)/shard_map/pallas_call | solution.py:458

commit v3 on v2

--- a/solution.py
+++ b/solution.py
@@ -449,7 +449,7 @@
         ),
     )(acts, hidden, grads, bases_main, bases_down, moment_first, moment_second)
 
-    steps = 8
+    steps = 4
     cols = moment_first.shape[1]
     once = pl.Buffered(1)
     band = lambda: pl.BlockSpec((RANK // steps, cols), lambda i: (i, 0))

time: 204 us -> 203 us (level)
  no operation moved by 1% of the time
where the time goes in v3:
time: 203 us
  Pallas kernels  202 us (100%)
    pallas_call x1, Pallas kernels, local_block(): pl.pallas_call(gather_reduce, out_shape=(jax.ShapeDtypeStruct((6, D, RANK...  178 us
    pallas_call x1, Pallas kernels, local_block(): pl.pallas_call(moments_and_updates, grid=(steps,), out_shape=[jax.ShapeDt...  24 us

profile of v3, /device:TPU:11, one launch (start us, length us, event | category | flops | bytes accessed | tf_op | source)
XLA Modules:
  0.0 202.9 jit_solution(11154893091645504620)
XLA Ops:
  0.6 178.1 %shard_map.142 = (bf16[6,4096,256]{2,1,0:T(8,128)(2,1)}, bf16[7168,256]{1,0:T(8,128)(2,1)}, bf16[4,256,896]{2,1,0:T(8,128)(2,1)}, bf16[256,3584]{1,0:T(8,128)(2,1)}) custom-call(bf16[3,128,4096]{2,1,0:T(8,128)(2,1)} %acts.1, bf16[128,7168]{1,0:T(8,128)(2,1)} %hidden.1, bf16[128,28672]{1,0:T(8,128)(2,1)} %grads.1, bf16[6,512,256]{2,1,0:T(8,128)(2,1)} %bmain.1, ...), custom_call_target="tpu_custom_call" | custom-call | tf_op jit(solution)/shard_map/pallas_call | solution.py:418
  178.7 24.0 %shard_map.143 = (f32[256,3584]{1,0:T(8,128)}, f32[256,3584]{1,0:T(8,128)}, bf16[4096,512]{1,0:T(8,128)(2,1)}, bf16[4096,128]{1,0:T(8,128)(2,1)}, bf16[4096,128]...) custom-call(bf16[4,256,896]{2,1,0:T(8,128)(2,1)} %get-tuple-element., ...), custom_call_target="tpu_custom_call" | custom-call | tf_op jit(solution)/shard_map/pallas_call | solution.py:458
